TPU v7x, 32 devices: a whole 2x2x4 slice. The times are simulated.
32 devices in a mesh: runs: 2 (over y), gx: 4 (over z), gy: 2 (over x), wa: 2 (over core).
Axes of the slice: x: 2, y: 2, z: 4, core: 2. Of those that a mesh axis runs over, the one named last changes fastest.
Arguments:
- slabs: float32 [6, 16, 256, 1024], P('runs', 'wa', 'gx', 'gy'), parts along dimension 0, may hold values from -6 to 6
- slab_index: int32 [6], P('runs'), parts along dimension 0, may hold values from 0 to 31
- omega_x: float32 [256, 64], P('gx'), may hold values from -0.375 to 0.375
- omega_y: float32 [1024, 64], P('gy'), may hold values from -0.1875 to 0.1875
- omega_z: float32 [512, 64], replicated, may hold values from -1.5 to 1.5
- phi_x: float32 [256, 128], P('gx'), may hold values from -0.375 to 0.375
- phi_y: float32 [1024, 128], P('gy'), may hold values from -0.1875 to 0.1875
- phi_z: float32 [512, 64], replicated, may hold values from -1.5 to 1.5
- sketch_x: float32 [512, 64], P(('runs', 'gx')), parts along dimension 0, may hold values from -6 to 6
- sketch_y: float32 [2048, 64], P(('runs', 'gy')), parts along dimension 0, may hold values from -6 to 6
- sketch_z: float32 [1024, 64], P('runs'), parts along dimension 0, may hold values from -6 to 6
- core: float32 [128, 128, 128], P(('runs', 'wa'), 'gx', 'gy'), parts along dimension 0, may hold values from -6 to 6
Outputs:
- new_sketch_x: float32 [512, 64], P(('runs', 'gx')), parts along dimension 0
- new_sketch_y: float32 [2048, 64], P(('runs', 'gy')), parts along dimension 0
- new_sketch_z: float32 [1024, 64], P('runs'), parts along dimension 0
- new_core: float32 [128, 128, 128], P(('runs', 'wa'), 'gx', 'gy'), parts along dimension 0
There are 2 independent parts, one for each index of `runs`. A program takes and returns all parts, laid end to end along the dimension named above; an argument that names none is the same for every part. Nothing has to cross between parts.
Inputs may be any that keep to these rules, and one draw needn't show every extreme that they name: `slab_index`: steps may bring the same slab more than once.
All inputs are finite; a program needn't handle non-finite values.
Results may differ from a plain program's by a relative error of at most 0.0001.
Values sent between devices are 32-bit elements; how exact they have to be, the bound alone decides.
A program may use at most 64 MiB of HBM per device.

v0:
```python
import jax
import jax.numpy as jnp
from jax import lax
from jax.sharding import PartitionSpec as P

DZ = 16


def contract(form, left, right):
    return jnp.einsum(form, left, right, precision=lax.Precision.HIGHEST)


def shards(
    slabs,
    slab_index,
    omega_x,
    omega_y,
    omega_z,
    phi_x,
    phi_y,
    phi_z,
    sketch_x,
    sketch_y,
    sketch_z,
    core,
):
    planes = slabs.shape[1]
    x_parts = lax.axis_size("gx")
    y_parts = lax.axis_size("gy")
    full_size = phi_x.shape[1]
    row_width = full_size // x_parts
    col_width = full_size // y_parts
    for step in range(slabs.shape[0]):
        field = slabs[step]
        first = slab_index[step] * DZ
        start = first + lax.axis_index("wa") * planes
        depth_omega = lax.dynamic_slice_in_dim(omega_z, start, planes, 0)
        depth_phi = lax.dynamic_slice_in_dim(phi_z, start, planes, 0)
        row_mix = contract("zij,jr->zir", field, omega_y)
        rows_part = contract("zir,zr->ir", row_mix, depth_omega)
        plane_part = contract("zir,ir->zr", row_mix, omega_x)
        col_mix = contract("zij,ir->zjr", field, omega_x)
        cols_part = contract("zjr,zr->jr", col_mix, depth_omega)
        core_cols = contract("zij,jb->zib", field, phi_y)
        sketch_x = sketch_x + lax.psum(rows_part, ("gy", "wa"))
        sketch_y = sketch_y + lax.psum(cols_part, ("gx", "wa"))
        plane_total = lax.psum(plane_part, ("gx", "gy"))
        slab_rows = lax.all_gather(plane_total, "wa", axis=0, tiled=True)
        current = lax.dynamic_slice_in_dim(sketch_z, first, DZ, 0)
        sketch_z = lax.dynamic_update_slice_in_dim(sketch_z, current + slab_rows, first, 0)
        core_both = contract("zib,ia->zab", core_cols, phi_x)
        blocks = core_both.reshape(planes, x_parts, row_width, y_parts, col_width)
        blocks = blocks.transpose(1, 3, 0, 2, 4).reshape(
            x_parts * y_parts * planes, row_width, col_width
        )
        owned = lax.psum_scatter(blocks, ("gx", "gy"), scatter_dimension=0, tiled=True)
        depth_term = contract("zab,zc->cab", owned, depth_phi)
        core = core + lax.psum_scatter(depth_term, "wa", scatter_dimension=0, tiled=True)
    return (sketch_x, sketch_y, sketch_z, core)


def solution(mesh):
    placed = (
        P("runs", "wa", "gx", "gy"),
        P("runs"),
        P("gx", None),
        P("gy", None),
        P(),
        P("gx", None),
        P("gy", None),
        P(),
        P(("runs", "gx"), None),
        P(("runs", "gy"), None),
        P("runs", None),
        P(("runs", "wa"), "gx", "gy"),
    )
    return jax.shard_map(
        shards,
        mesh=mesh,
        in_specs=placed,
        out_specs=(
            P(("runs", "gx"), None),
            P(("runs", "gy"), None),
            P("runs", None),
            P(("runs", "wa"), "gx", "gy"),
        ),
        check_vma=False,
    )
```

profile of v0, /device:TPU:0, one launch (start us, length us, event | category | flops | bytes accessed | tf_op | source)
XLA Modules:
  0.0 263.4 jit_solution(12916286075879260712)
XLA Ops:
  9.0 2.2 fusion.6
  11.2 2.7 %convolution_bitcast_fusion.1 = f32[8,128,128]{1,2,0:T(8,128)} fusion(f32[8,64,128]{2,1,0:T(8,128)S(1)} %fusion.6, f32[64,128]{1,0:T(8,128)} %param.17), kind=kOutput, calls=%fused_computation.1 | convolution fusion | flops 100663296 | bytes 819200 | tf_op jit(solution)/shard_map/zib,ia->zab/dot_general | solution.py:10
  13.9 2.1 copy.60
  15.9 2.6 reshape.34
  18.6 2.4 copy.61
  25.9 2.6 reshape.36
  28.5 2.4 copy.65
  35.8 2.6 %reshape.32 = f32[8,4,32,2,64]{4,3,2,1,0:T(2,128)} reshape(f32[8,128,128]{2,1,0:T(8,128)} %copy.55) | data formatting | bytes 1048576 | tf_op jit(solution)/shard_map/reshape | solution.py:52
  38.4 2.3 copy.56
  43.6 2.1 fusion.8
  45.7 2.1 fusion.14
  48.7 2.7 %fusion.22 = f32[64,1,512]{2,1,0:T(1,128)S(1)} fusion(f32[8,64,1]{0,2,1:T(1,128)S(1)} %bitcast.154, f32[8,512,64]{1,2,0:T(8,128)} %fusion.14), kind=kOutput, calls=%fused_computation.25 | convolution fusion | flops 3145728 | bytes 1181696 | tf_op jit(solution)/shard_map/zjr,zr->jr/dot_general | solution.py:10
  52.1 2.7 %fusion.20 = f32[64,1,512]{2,1,0:T(1,128)S(1)} fusion(f32[8,64,1]{0,2,1:T(1,128)S(1)} %bitcast.152, f32[8,512,64]{1,2,0:T(8,128)} %fusion.8), kind=kOutput, calls=%fused_computation.23 | convolution fusion | flops 3145728 | bytes 1181696 | tf_op jit(solution)/shard_map/zjr,zr->jr/dot_general | solution.py:10
  58.4 29.0 %reduce-scatter.11.cloned.1.call-done = f32[8,32,64]{2,1,0:T(8,128)} async-done(((f32[64,32,64]{2,1,0:T(8,128)}), f32[8,32,64]{2,1,0:T(8,128)}) %reduce-scatter.11.cloned.1.call-update) | async-done | bytes 65552 | tf_op jit(solution)/shard_map/reduce_scatter | solution.py:56
  87.3 3.0 %fusion.43 = f32[64,32,64]{2,0,1:T(8,128)} fusion(f32[8,32,64]{2,1,0:T(8,128)} %reduce-scatter.11.cloned.1.call-done, f32[512,64]{0,1:T(8,128)} %param.19, s32[]{:T(128)S(6)} %select_n.25), kind=kOutput, calls=%fused_computation.56 | convolution fusion | flops 12582912 | bytes 688132 | tf_op jit(solution)/shard_map/zab,zc->cab/dot_general | solution.py:10
  91.2 62.3 %reduce-scatter.15.cloned.1.call-done = f32[8,32,64]{2,1,0:T(8,128)} async-done(((f32[64,32,64]{2,1,0:T(8,128)}), f32[8,32,64]{2,1,0:T(8,128)}) %reduce-scatter.15.cloned.1.call-update) | async-done | bytes 65552 | tf_op jit(solution)/shard_map/reduce_scatter | solution.py:56
  153.5 2.9 %fusion.41 = f32[64,32,64]{2,0,1:T(8,128)} fusion(f32[8,32,64]{2,1,0:T(8,128)} %reduce-scatter.15.cloned.1.call-done, f32[512,64]{0,1:T(8,128)} %param.19, s32[]{:T(128)S(6)} %select_n.26), kind=kOutput, calls=%fused_computation.54 | convolution fusion | flops 12582912 | bytes 688132 | tf_op jit(solution)/shard_map/zab,zc->cab/dot_general | solution.py:10
  156.7 2.3 multiply_reduce_fusion.5
  166.7 35.2 %all-reduce.1 = (f32[8,64]{1,0:T(8,128)S(1)}, f32[8,64]{1,0:T(8,128)S(1)}, f32[8,64]{1,0:T(8,128)S(1)}) all-reduce(f32[8,64]{1,0:T(8,128)S(1)} %bitcast.161, f32[8,64]{1,0:T(8,128)S(1)} %bitcast.160, f32[8,64]{1,0:T(8,128)S(1)} %bitcast.159), channel_id=1, replica_groups=mesh['runs'=2,'gx'=4,'gy'=2,'wa'=2] {'gx','gy'}, use_global_device_ids=true, to_apply=%region_6.0 | all-reduce | flops 1536 | bytes 12288 | tf_op jit(solution)/shard_map/psum | solution.py:47
  207.3 12.4 %reduce-scatter.7.cloned.1.call-done = f32[8,32,64]{2,1,0:T(8,128)} async-done(((f32[64,32,64]{2,1,0:T(8,128)}), f32[8,32,64]{2,1,0:T(8,128)}) %reduce-scatter.7.cloned.1.call-update) | async-done | bytes 65552 | tf_op jit(solution)/shard_map/reduce_scatter | solution.py:56
  219.7 2.9 %fusion.45 = f32[64,32,64]{2,0,1:T(8,128)} fusion(f32[8,32,64]{2,1,0:T(8,128)} %reduce-scatter.7.cloned.1.call-done, f32[512,64]{0,1:T(8,128)} %param.19, s32[]{:T(128)S(6)} %select_n.24), kind=kOutput, calls=%fused_computation.58 | convolution fusion | flops 12582912 | bytes 688132 | tf_op jit(solution)/shard_map/zab,zc->cab/dot_general | solution.py:10
  223.5 11.1 %all-reduce.2 = (f32[64,64]{1,0:T(8,128)S(1)}, f32[64,64]{1,0:T(8,128)S(1)}, f32[64,64]{1,0:T(8,128)S(1)}) all-reduce(f32[64,64]{1,0:T(8,128)S(1)} %bitcast.157, f32[64,64]{1,0:T(8,128)S(1)} %bitcast.158, f32[64,64]{1,0:T(8,128)S(1)} %bitcast.156), channel_id=1, replica_groups=mesh['runs'=2,'gx'=4,'gy'=2,'wa'=2] {'gy','wa'}, use_global_device_ids=true, to_apply=%region_2.0 | all-reduce | flops 12288 | bytes 98304 | tf_op jit(solution)/shard_map/psum | solution.py:45
  237.0 4.3 %reduce-scatter.17.cloned.1.call-done = f32[32,32,64]{2,0,1:T(8,128)} async-done(((f32[64,32,64]{2,0,1:T(8,128)}), f32[32,32,64]{2,0,1:T(8,128)}) %reduce-scatter.17.cloned.1.call-update) | async-done | bytes 262160 | tf_op jit(solution)/shard_map/reduce_scatter | solution.py:58
  241.3 11.8 %reduce-scatter.9.cloned.1.call-done = f32[32,32,64]{2,0,1:T(8,128)} async-done(((f32[64,32,64]{2,0,1:T(8,128)}), f32[32,32,64]{2,0,1:T(8,128)}) %reduce-scatter.9.cloned.1.call-update) | async-done | bytes 262160 | tf_op jit(solution)/shard_map/reduce_scatter | solution.py:58
  (78 shorter events, 36.8 us)
Async XLA Ops:
  8.0 1.0 copy-start
  8.0 79.3 %reduce-scatter.11.cloned.1.call-start = ((), (), s32[]{:S(2)}) async-start(), calls=%async_computation.8 | async-start | bytes 1179648 | tf_op jit(solution)/shard_map/reduce_scatter | solution.py:56
  11.2 9.9 %copy-start.1 = (f32[3,8,64,512]{3,2,1,0:T(8,128)S(1)}, f32[3,8,64,512]{3,2,1,0:T(8,128)}, u32[]{:S(2)}) copy-start(f32[3,8,64,512]{3,2,1,0:T(8,128)} %param.12) | copy-start | bytes 9437188
  15.9 6.1 %copy-start.6 = (f32[64,128]{1,0:T(8,128)S(1)}, f32[64,128]{1,0:T(8,128)}, u32[]{:S(2)}) copy-start(f32[64,128]{1,0:T(8,128)} %param.17) | copy-start | bytes 98308
  21.0 132.5 %reduce-scatter.15.cloned.1.call-start = ((), (), s32[]{:S(2)}) async-start(), calls=%async_computation.10 | async-start | bytes 1179648 | tf_op jit(solution)/shard_map/reduce_scatter | solution.py:56
  30.9 188.8 %reduce-scatter.7.cloned.1.call-start = ((), (), s32[]{:S(2)}) async-start(), calls=%async_computation.6 | async-start | bytes 1179648 | tf_op jit(solution)/shard_map/reduce_scatter | solution.py:56
  31.9 9.1 %copy-start.15 = (s32[3]{0:T(128)S(1)}, s32[3]{0:T(128)}, u32[]{:S(2)}) copy-start(s32[3]{0:T(128)} %param.13) | copy-start | bytes 40
  31.9 11.6 %copy-start.4 = (f32[64,64]{1,0:T(8,128)S(1)}, f32[64,64]{1,0:T(8,128)}, u32[]{:S(2)}) copy-start(f32[64,64]{1,0:T(8,128)} %param.14) | copy-start | bytes 49156
  40.8 194.5 %all-reduce.5.cloned.1.call-start = ((), (), s32[]{:S(2)}) async-start(), calls=%async_computation.12 | async-start | bytes 786432 | tf_op jit(solution)/shard_map/psum | solution.py:46
  48.7 7.3 %copy-start.8 = (f32[8,64]{0,1:T(8,128)}, f32[8,64]{0,1:T(8,128)S(1)}, u32[]{:S(2)}) copy-start(f32[8,64]{0,1:T(8,128)S(1)} %get-tuple-element.34) | copy-start | bytes 6148
  48.7 7.3 %copy-start.9 = (f32[8,64]{0,1:T(8,128)}, f32[8,64]{0,1:T(8,128)S(1)}, u32[]{:S(2)}) copy-start(f32[8,64]{0,1:T(8,128)S(1)} %get-tuple-element.32) | copy-start | bytes 6148
  48.7 9.6 %copy-start.7 = (f32[8,64]{0,1:T(8,128)}, f32[8,64]{0,1:T(8,128)S(1)}, u32[]{:S(2)}) copy-start(f32[8,64]{0,1:T(8,128)S(1)} %get-tuple-element.33) | copy-start | bytes 6148
  56.0 100.7 %copy-start.2 = (f32[512,64]{0,1:T(8,128)S(1)}, f32[512,64]{0,1:T(8,128)}, u32[]{:S(2)}) copy-start(f32[512,64]{0,1:T(8,128)} %param.15) | copy-start | bytes 393220
  58.3 178.7 %reduce-scatter.13.cloned.1.call-start = ((), (), s32[]{:S(2)}) async-start(), calls=%async_computation.9 | async-start | bytes 1572864 | tf_op jit(solution)/shard_map/reduce_scatter | solution.py:58
  90.3 151.0 %reduce-scatter.17.cloned.1.call-start = ((), (), s32[]{:S(2)}) async-start(), calls=%async_computation.11 | async-start | bytes 1572864 | tf_op jit(solution)/shard_map/reduce_scatter | solution.py:58
  156.4 96.7 %reduce-scatter.9.cloned.1.call-start = ((), (), s32[]{:S(2)}) async-start(), calls=%async_computation.7 | async-start | bytes 1572864 | tf_op jit(solution)/shard_map/reduce_scatter | solution.py:58
  165.5 57.1 %copy-start.3 = (f32[512,64]{1,0:T(8,128)S(1)}, f32[512,64]{1,0:T(8,128)}, u32[]{:S(2)}) copy-start(f32[512,64]{1,0:T(8,128)} %copy.53) | copy-start | bytes 393220
  165.5 57.9 %copy-start.11 = (f32[64,64]{0,1:T(8,128)S(1)}, f32[64,64]{0,1:T(8,128)}, u32[]{:S(2)}) copy-start(f32[64,64]{0,1:T(8,128)} %get-tuple-element.42) | copy-start | bytes 49156
  165.5 57.9 %copy-start.12 = (f32[64,64]{0,1:T(8,128)S(1)}, f32[64,64]{0,1:T(8,128)}, u32[]{:S(2)}) copy-start(f32[64,64]{0,1:T(8,128)} %get-tuple-element.38) | copy-start | bytes 49156
  165.5 57.9 %copy-start.13 = (f32[64,64]{0,1:T(8,128)S(1)}, f32[64,64]{0,1:T(8,128)}, u32[]{:S(2)}) copy-start(f32[64,64]{0,1:T(8,128)} %get-tuple-element.40) | copy-start | bytes 49156
  165.5 69.1 %copy-start.14 = (f32[64,64]{1,0:T(8,128)S(1)}, f32[64,64]{1,0:T(8,128)}, u32[]{:S(2)}) copy-start(f32[64,64]{1,0:T(8,128)} %param.20) | copy-start | bytes 49156
  165.6 69.7 %copy-start.10 = (f32[512,64]{0,1:T(8,128)S(1)}, f32[512,64]{0,1:T(8,128)}, u32[]{:S(2)}) copy-start(f32[512,64]{0,1:T(8,128)} %param.21) | copy-start | bytes 393220
  165.6 87.5 %copy-start.5 = (f32[32,32,64]{2,1,0:T(8,128)S(1)}, f32[32,32,64]{2,1,0:T(8,128)}, u32[]{:S(2)}) copy-start(f32[32,32,64]{2,1,0:T(8,128)} %param.23) | copy-start | bytes 786436
Sparse Core Ops, SparseCore 0:
  21.1 66.2 reduce-scatter.10
  90.8 62.6 reduce-scatter.14
  157.3 62.4 reduce-scatter.6
  221.8 7.5 reduce-scatter.12
  231.6 9.6 reduce-scatter.16
  243.4 9.6 reduce-scatter.8
Sparse Core Ops, SparseCore 1:
  58.4 60.2 all-reduce.4
where the time goes:
time: 265 us; the launch traced here: 263 us
  waiting for transfers between devices  120 us (45%)
  blocking collectives  51.7 us (20%)
  matrix products  37 us (14%)
  local copies, waits for them, and re-layouts  31 us (12%)
  between operations  17.8 us (7%)
  other arithmetic  5.28 us (2%)
    reduce_scatter x3, waiting for transfers between devices, shards(): lax.psum_scatter(blocks, ('gx', 'gy'), scatter_dimension=0, tiled=True)  104 us
    dot_general x18, matrix products, contract(): return jnp.einsum(form, left, right, precision=lax.Precision.HIGHEST)  37 us
    psum x1, blocking collectives, shards(): plane_total = lax.psum(plane_part, ('gx', 'gy'))  35.2 us
    reduce_scatter x3, waiting for transfers between devices, shards(): lax.psum_scatter(depth_term, 'wa', scatter_dimension=0, tiled=True)  16.1 us
    psum x1, blocking collectives, shards(): sketch_x = sketch_x + lax.psum(rows_part, ('gy', 'wa'))  11.1 us
    reshape x3, local copies, waits for them, and re-layouts, shards(): blocks = core_both.reshape(planes, x_parts, row_width, y_parts, col_width)  7.89 us
    transpose x3, local copies, waits for them, and re-layouts, shards(): blocks.transpose(1, 3, 0, 2, 4)  7.08 us
    unnamed x38, local copies, waits for them, and re-layouts  7.07 us
  transfers between devices with their start and end apart: 7, of which 5 were waited for; matrix products, arithmetic and copies ran while one was open for 22% of the time, Pallas kernels for 0%

commit v1 on v0

--- a/solution.py
+++ b/solution.py
@@ -1,28 +1,437 @@
+import functools
+
 import jax
 import jax.numpy as jnp
 from jax import lax
+from jax.experimental import pallas as pl
+from jax.experimental.pallas import tpu as pltpu
 from jax.sharding import PartitionSpec as P
 
 DZ = 16
+F32 = jnp.float32
+BF16 = jnp.bfloat16
+LANES = 128
+NN = (((1,), (0,)), ((), ()))
+NT = (((1,), (1,)), ((), ()))
 
 
 def contract(form, left, right):
     return jnp.einsum(form, left, right, precision=lax.Precision.HIGHEST)
 
 
-def shards(
-    slabs,
-    slab_index,
-    omega_x,
-    omega_y,
-    omega_z,
-    phi_x,
-    phi_y,
-    phi_z,
-    sketch_x,
-    sketch_y,
-    sketch_z,
-    core,
+def split(value):
+    high = value.astype(BF16)
+    return high, (value - high.astype(F32)).astype(BF16)
+
+
+def mul(left, right, dims=NN):
+    return lax.dot_general(left, right, dims, preferred_element_type=F32)
+
+
+def mul3(left_high, left_low, right_high, right_low, dims=NN):
+    rows = left_high.shape[0]
+    both = mul(jnp.concatenate([left_high, left_low], axis=0), right_high, dims)
+    return both[:rows] + both[rows:] + mul(left_high, right_low, dims)
+
+
+def iota(shape, dim):
+    return lax.broadcasted_iota(jnp.int32, shape, dim)
+
+
+def fused(
+    steps, planes, rows, row_width, col_width,
+    index, slabs, omega_x, omega_y, omega_z, phi_x, phi_y, phi_z, sketch_x, sketch_y, sketch_z, core,
+    new_x, new_y, new_z, new_core,
+    v_slabs, v_ox, v_oy, v_oz, v_px, v_py, v_pz, v_sx, v_sy, v_sz, v_core, in_sem,
+    gy_out, gy_in, cols, px_in, raw_in, keep, mid_out, mid_in, end_out, end_in, total, wa_in,
+    mix, own_high, own_low, far_high, far_low, y_sum, x_sum, z_sum, hot, depth,
+    g1_out, g1_in, g2_out, g2_in, ga_out, ga_in, gb_out, gb_in, gc_in, g4_out, g4_in, cube,
+    o_x, o_y, o_z, o_core, out_sem, send_sem, recv_sem,
+):
+    gx, gy, wa = lax.axis_index("gx"), lax.axis_index("gy"), lax.axis_index("wa")
+    pair = gx + 1 - 2 * lax.rem(gx, 2)
+    across = 3 - gx
+    inner = jnp.logical_or(gx == 1, gx == 2)
+    outer = jnp.logical_not(inner)
+    group = LANES // row_width
+    quads = planes // group
+    full = v_px.shape[1]
+    rank = v_oy.shape[0]
+    half = rank // 2
+    n_sems = [0]
+
+    def local(src, dst, sem):
+        return pltpu.make_async_copy(src, dst, sem)
+
+    sources = (phi_y, omega_y, omega_z, omega_x, phi_x, phi_z, sketch_x, sketch_y, sketch_z, core)
+    places = (v_py, v_oy, v_oz, v_ox, v_px, v_pz, v_sx, v_sy, v_sz, v_core)
+    loads = [local(s, d, in_sem.at[k]) for k, (s, d) in enumerate(zip(sources, places))]
+    fields = [local(slabs.at[t], v_slabs.at[t], in_sem.at[len(loads) + t]) for t in range(steps)]
+    for copy in loads[:2] + fields[:1] + loads[2:6] + fields[1:] + loads[6:]:
+        copy.start()
+
+    barrier = pltpu.get_barrier_semaphore()
+    for where in ({"wa": 1 - wa}, {"gy": 1 - gy}, {"gx": pair}):
+        pl.semaphore_signal(barrier, inc=1, device_id=where, device_id_type=pl.DeviceIdType.MESH)
+
+    @pl.when(inner)
+    def _():
+        pl.semaphore_signal(barrier, inc=1, device_id={"gx": across}, device_id_type=pl.DeviceIdType.MESH)
+
+    def remote(src, dst, where):
+        k = n_sems[0]
+        n_sems[0] += 1
+        return pltpu.make_async_remote_copy(
+            src_ref=src, dst_ref=dst, send_sem=send_sem.at[k], recv_sem=recv_sem.at[k],
+            device_id=where, device_id_type=pl.DeviceIdType.MESH,
+        )
+
+    to_gy = [remote(gy_out.at[t], gy_in.at[t], {"gy": 1 - gy}) for t in range(steps)]
+    to_px = remote(v_px, px_in, {"gx": pair})
+    to_raw = [remote(cols.at[t], raw_in.at[t], {"gx": pair}) for t in range(steps)]
+    to_mid = [remote(mid_out.at[t], mid_in.at[t], {"gx": across}) for t in range(steps)]
+    to_end = [remote(end_out.at[t], end_in.at[t], {"gx": pair}) for t in range(steps)]
+    to_wa = [remote(total.at[t], wa_in.at[t], {"wa": 1 - wa}) for t in range(steps)]
+    to_g1 = remote(g1_out, g1_in, {"wa": 1 - wa})
+    to_g2 = remote(g2_out, g2_in, {"gy": 1 - gy})
+    to_ga = remote(ga_out, ga_in, {"gx": pair})
+    to_gb = remote(gb_out, gb_in, {"gx": across})
+    to_gc = remote(g4_out, gc_in, {"gx": pair})
+    to_g4 = remote(g4_out, g4_in, {"wa": 1 - wa})
+
+    loads[0].wait()
+    loads[1].wait()
+    for k, part in enumerate(split(jnp.concatenate([v_py[...].T, v_oy[...]], axis=0))):
+        mix[k] = part
+
+    loads[2].wait()
+    loads[3].wait()
+    loads[4].wait()
+    loads[5].wait()
+    depth_count = steps * planes
+
+    def rows_of(offsets):
+        lane = iota((v_oz.shape[1], LANES), 1)
+        wanted = jnp.full(lane.shape, -1, jnp.int32)
+        for k, offset in enumerate(offsets):
+            for t in range(steps):
+                first = k * depth_count + t * planes
+                inside = jnp.logical_and(lane >= first, lane < first + planes)
+                wanted = jnp.where(inside, lane - first + (index[t] * DZ + offset), wanted)
+        return (iota(lane.shape, 0) == wanted).astype(BF16)
+
+    here, there = wa * planes, (1 - wa) * planes
+    hot[0] = rows_of((here, there))
+    hot[1] = rows_of((there,))
+    oz_high, oz_low = (mul(part, hot[0]).astype(BF16) for part in split(v_oz[...]))
+    for k, part in enumerate(split(v_pz[...])):
+        depth[k] = mul(part, hot[0])
+    ox_t = v_ox[...].T
+    ox_tiles = jnp.concatenate([ox_t] * planes, axis=1)
+    def compute(t):
+        fields[t].wait()
+        x_high, x_low = split(v_slabs[t])
+        mixed = mul3(mix[0], mix[1], x_high, x_low, NT)
+        for k in range(2):
+            @pl.when(gy == k)
+            def _():
+                cols[t] = mixed[k * col_width:(k + 1) * col_width]
+                gy_out[t] = mixed[(1 - k) * col_width:(2 - k) * col_width]
+        row_mix = mixed[full:]
+        shape = (LANES, planes * rows)
+        spread = (iota(shape, 0) == t * planes + iota(shape, 1) // rows).astype(BF16)
+        weight = mul(oz_high, spread) + mul(oz_low, spread)
+        w_high, w_low = split(weight * ox_tiles)
+        y_part = mul3(w_high, w_low, x_high, x_low)
+        weighted = row_mix * weight
+        x_part = functools.reduce(
+            jnp.add, [weighted[:, k:k + LANES] for k in range(0, planes * rows, LANES)]
+        )
+        m_high, m_low = split(row_mix * ox_tiles)
+        z_part = mul(m_high, spread, NT) + mul(m_low, spread, NT)
+        if t == 0:
+            y_sum[...] = y_part
+            x_sum[...] = x_part
+            z_sum[...] = z_part
+        else:
+            y_sum[...] += y_part
+            x_sum[...] += x_part
+            z_sum[...] += z_part
+
+    def blocks_of(phi, high_ref, low_ref):
+        phi_high, phi_low = split(phi)
+        k, l = iota((full, LANES), 0), iota((full, LANES), 1)
+        owners = (gx, pair, across, across + 1 - 2 * lax.rem(across, 2))
+        same = iota((group * rows, LANES), 0) // rows == iota((group * rows, LANES), 1) // row_width
+        for o, owner in enumerate(owners):
+            chosen = (k == owner * row_width + lax.rem(l, row_width)).astype(BF16)
+            for part, ref in ((phi_high, high_ref), (phi_low, low_ref)):
+                tiled = jnp.concatenate([mul(part, chosen)] * group, axis=0)
+                ref[:, o * LANES:(o + 1) * LANES] = jnp.where(same, tiled, 0.0).astype(BF16)
+
+    def apply_x(value, high_ref, low_ref):
+        stacked = jnp.concatenate(
+            [value[:, q * group * rows:(q + 1) * group * rows] for q in range(quads)], axis=0
+        )
+        high, low = split(stacked)
+        return mul3(high, low, high_ref[...], low_ref[...])
+
+    compute(0)
+
+    @pl.when(inner)
+    def _():
+        pl.semaphore_wait(barrier, 4)
+
+    @pl.when(outer)
+    def _():
+        pl.semaphore_wait(barrier, 3)
+
+    to_gy[0].start()
+
+    @pl.when(outer)
+    def _():
+        to_px.start()
+
+    for t in range(1, steps):
+        compute(t)
+        to_gy[t].start()
+
+    for k in range(2):
+        @pl.when(wa == k)
+        def _():
+            g1_out[0:half, :] = y_sum[(1 - k) * half:(2 - k) * half, :]
+    fold = rank // 4
+    for k in range(4):
+        g1_out[half:half + fold, k * LANES:(k + 1) * LANES] = x_sum[k * fold:(k + 1) * fold, :]
+    to_g1.start()
+
+    @pl.when(inner)
+    def _():
+        blocks_of(v_px[...], own_high, own_low)
+        to_px.wait_recv()
+        blocks_of(px_in[...], far_high, far_low)
+
+    def stage_b(t):
+        to_gy[t].wait_recv()
+        summed = cols[t] + gy_in[t]
+
+        cols[t] = summed
+
+        @pl.when(outer)
+        def _():
+            to_raw[t].start()
+
+        @pl.when(inner)
+        def _():
+            keep[t] = apply_x(cols[t], own_high, own_low)
+
+    def stage_c(t):
+        @pl.when(inner)
+        def _():
+            to_raw[t].wait_recv()
+            both = keep[t] + apply_x(raw_in[t], far_high, far_low)
+            keep[t] = both
+            mid_out[t] = both[:, 2 * LANES:]
+            to_mid[t].start()
+
+    def stage_d(t):
+        @pl.when(inner)
+        def _():
+            to_mid[t].wait_recv()
+            end_out[t] = keep[t, :, LANES:2 * LANES] + mid_in[t, :, LANES:]
+            to_end[t].start()
+            total[t] = keep[t, :, :LANES] + mid_in[t, :, :LANES]
+
+    def stage_e(t):
+        @pl.when(outer)
+        def _():
+            to_end[t].wait_recv()
+            total[t] = end_in[t]
+        to_wa[t].start()
+        turn(0, t, total)
+
+    def turn(which, t, ref):
+        for q in range(quads):
+            first = (which * steps + t) * planes * row_width + q * LANES
+            cube[first:first + LANES, :] = ref[t, q * col_width:(q + 1) * col_width, :].T
+
+    def stage_f(t):
+        to_wa[t].wait_recv()
+        turn(1, t, wa_in)
+
+    def g1():
+        to_g1.wait_recv()
+        for k in range(2):
+            @pl.when(wa == k)
+            def _():
+                ga_out[0:half, :] = y_sum[k * half:(k + 1) * half, :] + g1_in[0:half, :]
+        g2_out[0:fold, :] = g1_out[half:half + fold, :] + g1_in[half:half + fold, :]
+        for k in range(4):
+            g2_out[fold:, k * LANES:(k + 1) * LANES] = z_sum[k * fold:(k + 1) * fold, :]
+        to_g2.start()
+
+    def g2():
+        to_g2.wait_recv()
+        ga_out[half:, :] = g2_out[fold:, :] + g2_in[fold:, :]
+
+        @pl.when(outer)
+        def _():
+            to_ga.start()
+
+        x_all = g2_out[0:fold, :] + g2_in[0:fold, :]
+        x_all = jnp.concatenate([x_all[:, k * LANES:(k + 1) * LANES] for k in range(4)], axis=0)
+        loads[6].wait()
+        o_x[...] = v_sx[...] + (x_all[:, :rows] + x_all[:, rows:]).T
+        local(o_x, new_x, out_sem.at[0]).start()
+
+    def g3():
+        @pl.when(inner)
+        def _():
+            to_ga.wait_recv()
+            gb_out[...] = ga_out[...] + ga_in[...]
+            to_gb.start()
+
+    def g4():
+        @pl.when(inner)
+        def _():
+            to_gb.wait_recv()
+            g4_out[...] = gb_out[...] + gb_in[...]
+            to_gc.start()
+
+    def g5():
+        @pl.when(outer)
+        def _():
+            to_gc.wait_recv()
+            g4_out[...] = gc_in[...]
+        to_g4.start()
+
+    def g6():
+        to_g4.wait_recv()
+        loads[7].wait()
+        loads[8].wait()
+        for k in range(2):
+            @pl.when(wa == k)
+            def _():
+                lower, upper = (g4_out, g4_in) if k == 0 else (g4_in, g4_out)
+                o_y[0:half, :] = v_sy[0:half, :] + lower[0:half, :]
+                o_y[half:, :] = v_sy[half:, :] + upper[0:half, :]
+        value = v_sz[...]
+        for ref, places in ((g4_out, hot[0]), (g4_in, hot[1])):
+            added = [ref[half:, k * LANES:(k + 1) * LANES] for k in range(4)]
+            for part in split(jnp.concatenate(added, axis=0)):
+                value = value + mul(part, places, NT)
+        o_z[...] = value
+        local(o_y, new_y, out_sem.at[1]).start()
+        local(o_z, new_z, out_sem.at[2]).start()
+
+    stage_b(0)
+    g1()
+    stage_b(1)
+    stage_c(0)
+    g2()
+    stage_b(2)
+    stage_c(1)
+    stage_d(0)
+    g3()
+    stage_c(2)
+    stage_e(0)
+    stage_d(1)
+    g4()
+    stage_e(1)
+    g5()
+    stage_f(0)
+    stage_f(1)
+    stage_d(2)
+    g6()
+    stage_e(2)
+    stage_f(2)
+
+    loads[9].wait()
+    owned = v_pz.shape[0] // 2
+    count = 2 * depth_count
+    spot = pl.ds(pl.multiple_of(wa * owned, owned), owned)
+    p_high, p_low = (depth[k, spot, :][:, :count].astype(BF16) for k in range(2))
+    for a in range(row_width):
+        high, low = split(cube[pl.ds(a, count, stride=row_width), :])
+        spot = pl.ds(a, owned, stride=row_width)
+        o_core[spot, :] = v_core[spot, :] + mul3(p_high, p_low, high, low)
+    local(o_core, new_core, out_sem.at[3]).start()
+
+    for copy in to_gy + to_wa + [to_g1, to_g2, to_g4]:
+        copy.wait_send()
+
+    @pl.when(outer)
+    def _():
+        for copy in to_raw + [to_px, to_ga]:
+            copy.wait_send()
+
+    @pl.when(inner)
+    def _():
+        for copy in to_mid + to_end + [to_gb, to_gc]:
+            copy.wait_send()
+
+    for k, (src, dst) in enumerate(((o_x, new_x), (o_y, new_y), (o_z, new_z), (o_core, new_core))):
+        local(src, dst, out_sem.at[k]).wait()
+
+
+def one_kernel(
+    slabs, slab_index, omega_x, omega_y, omega_z, phi_x, phi_y, phi_z, sketch_x, sketch_y, sketch_z, core
+):
+    steps, planes, rows, width = slabs.shape
+    rank, full = omega_x.shape[1], phi_x.shape[1]
+    row_width, col_width = core.shape[1], core.shape[2]
+    group = LANES // row_width
+    quads = planes // group
+    flat = planes * rows
+    half, fold = rank // 2, rank // 4
+    line = half + fold
+    vmem = lambda shape, kind=F32: pltpu.VMEM(shape, kind)
+    like = lambda value: vmem(value.shape)
+    flat_core = core.reshape(-1, col_width)
+    operands = (
+        slabs.reshape(steps, flat, width), omega_x, omega_y.T, omega_z.T, phi_x, phi_y, phi_z.T,
+        sketch_x, sketch_y.T, sketch_z.T, flat_core,
+    )
+    scratch = [like(value) for value in operands]
+    scratch += [
+        pltpu.SemaphoreType.DMA((10 + steps,)),
+        vmem((steps, col_width, flat)), vmem((steps, col_width, flat)), vmem((steps, col_width, flat)),
+        vmem((rows, full)), vmem((steps, col_width, flat)),
+        vmem((steps, quads * col_width, 4 * LANES)),
+        vmem((steps, quads * col_width, 2 * LANES)), vmem((steps, quads * col_width, 2 * LANES)),
+        vmem((steps, quads * col_width, LANES)), vmem((steps, quads * col_width, LANES)),
+        vmem((steps, quads * col_width, LANES)), vmem((steps, quads * col_width, LANES)),
+        vmem((2, full + rank, width), BF16),
+        vmem((group * rows, 4 * LANES), BF16), vmem((group * rows, 4 * LANES), BF16),
+        vmem((group * rows, 4 * LANES), BF16), vmem((group * rows, 4 * LANES), BF16),
+        vmem((rank, width)), vmem((rank, LANES)), vmem((rank, LANES)),
+        vmem((2, omega_z.shape[0], LANES), BF16), vmem((2, phi_z.shape[1], LANES)),
+        vmem((half + fold, width)), vmem((half + fold, width)),
+        vmem((2 * fold, width)), vmem((2 * fold, width)),
+        vmem((line, width)), vmem((line, width)), vmem((line, width)), vmem((line, width)),
+        vmem((line, width)), vmem((line, width)), vmem((line, width)),
+        vmem((2 * steps * planes * row_width, col_width)),
+        *(like(value) for value in operands[-4:]),
+        pltpu.SemaphoreType.DMA((4,)),
+        pltpu.SemaphoreType.DMA((5 * steps + 7,)),
+        pltpu.SemaphoreType.DMA((5 * steps + 7,)),
+    ]
+    outs = [jax.ShapeDtypeStruct(v.shape, F32) for v in operands[-4:]]
+    new_x, new_y, new_z, new_core = pl.pallas_call(
+        functools.partial(fused, steps, planes, rows, row_width, col_width),
+        out_shape=outs,
+        in_specs=[pl.BlockSpec(memory_space=pltpu.SMEM)] + [pl.BlockSpec(memory_space=pl.ANY)] * len(operands),
+        out_specs=[pl.BlockSpec(memory_space=pl.ANY)] * 4,
+        scratch_shapes=scratch,
+        compiler_params=pltpu.CompilerParams(
+            collective_id=0, has_side_effects=True, vmem_limit_bytes=48 * 2 ** 20
+        ),
+    )(slab_index, *operands)
+    return new_x, new_y.T, new_z.T, new_core.reshape(core.shape)
+
+
+def by_collectives(
+    slabs, slab_index, omega_x, omega_y, omega_z, phi_x, phi_y, phi_z, sketch_x, sketch_y, sketch_z, core
 ):
     planes = slabs.shape[1]
     x_parts = lax.axis_size("gx")
@@ -60,6 +469,8 @@
 
 
 def solution(mesh):
+    shape = dict(mesh.shape)
+    in_kernel = (shape["gx"], shape["gy"], shape["wa"]) == (4, 2, 2)
     placed = (
         P("runs", "wa", "gx", "gy"),
         P("runs"),
@@ -75,7 +486,7 @@
         P(("runs", "wa"), "gx", "gy"),
     )
     return jax.shard_map(
-        shards,
+        one_kernel if in_kernel else by_collectives,
         mesh=mesh,
         in_specs=placed,
         out_specs=(

time: 265 us -> 51.6 us (0.19)
  waiting for transfers between devices: 120 us -> 0 us
  blocking collectives: 51.7 us -> 0 us
  matrix products: 37 us -> 0 us
  Pallas kernels: 0 us -> 36.4 us
  between operations: 17.8 us -> 0.67 us
  local copies, waits for them, and re-layouts: 31 us -> 14 us
  other arithmetic: 5.28 us -> 0 us
    reduce_scatter x6 -> x0, waiting for transfers between devices: 120 us -> none  [the longest x3 104 us: shards(): lax.psum_scatter(blocks, ('gx', 'gy'), scatter_dimension=0, tiled=True)]
    psum x2 -> x0, blocking collectives: 46.3 us -> none  [the longest x1 35.2 us: shards(): plane_total = lax.psum(plane_part, ('gx', 'gy'))]
    dot_general x18 -> x0, matrix products: 37 us -> none  [contract(): return jnp.einsum(form, left, right, precision=lax.Precision.HIGHEST)]
    pallas_call x0 -> x1, Pallas kernels: none -> 36.4 us  [one_kernel(): pl.pallas_call(functools.partial(fused, steps, planes, rows, row_width, c...]
    transpose x7 -> x0, local copies, waits for them, and re-layouts: 13.9 us -> none  [the longest x3 7.08 us: shards(): blocks.transpose(1, 3, 0, 2, 4)]
    reshape x3 -> x0, local copies, waits for them, and re-layouts: 7.89 us -> none  [shards(): blocks = core_both.reshape(planes, x_parts, row_width, y_parts, col_width)]
    unnamed x38 -> x28, local copies, waits for them, and re-layouts: 7.07 us -> 14 us
    all_gather x3 -> x0, blocking collectives: 5.35 us -> none  [shards(): slab_rows = lax.all_gather(plane_total, 'wa', axis=0, tiled=True)]
  transfers between devices with their start and end apart: 7 -> 0, of which waited for: 5 -> 0; matrix products, arithmetic and copies ran while one was open for 22% -> 0% of each run, Pallas kernels for 0% -> 0%
where the time goes in v1:
time: 51.6 us; the launch traced here: 51.1 us
  Pallas kernels  36.4 us (71%)
  local copies, waits for them, and re-layouts  14 us (27%)
  between operations  0.67 us (1%)
    pallas_call x1, Pallas kernels, one_kernel(): pl.pallas_call(functools.partial(fused, steps, planes, rows, row_width, c...  36.4 us
    unnamed x28, local copies, waits for them, and re-layouts  14 us

profile of v1, /device:TPU:0, one launch (start us, length us, event | category | flops | bytes accessed | tf_op | source)
XLA Modules:
  0.0 51.1 jit_solution(6717165552314524276)
XLA Ops:
  0.6 0.0 copy-start
  0.6 1.9 %copy-done = f32[3,8,64,512]{3,2,1,0:T(8,128)S(1)} copy-done((f32[3,8,64,512]{3,2,1,0:T(8,128)S(1)}, f32[3,8,64,512]{3,2,1,0:T(8,128)}, u32[]{:S(2)}) %copy-start) | copy-done | bytes 3145752
  2.5 0.0 copy-start.1
  2.5 1.0 %copy-done.1 = f32[32,32,64]{2,1,0:T(8,128)S(1)} copy-done((f32[32,32,64]{2,1,0:T(8,128)S(1)}, f32[32,32,64]{2,1,0:T(8,128)}, u32[]{:S(2)}) %copy-start.1) | copy-done | bytes 262168
  3.6 0.0 copy-start.2
  3.6 0.9 %copy-done.2 = f32[512,128]{1,0:T(8,128)S(1)} copy-done((f32[512,128]{1,0:T(8,128)S(1)}, f32[512,128]{1,0:T(8,128)}, u32[]{:S(2)}) %copy-start.2) | copy-done | bytes 262168
  4.5 0.9 %copy-done.3 = f32[512,64]{0,1:T(8,128)S(1)} copy-done((f32[512,64]{0,1:T(8,128)S(1)}, f32[512,64]{0,1:T(8,128)}, u32[]{:S(2)}) %copy-start.3) | copy-done | bytes 131096
  5.4 0.0 copy-start.4
  5.4 0.9 %copy-done.4 = f32[512,64]{0,1:T(8,128)S(1)} copy-done((f32[512,64]{0,1:T(8,128)S(1)}, f32[512,64]{0,1:T(8,128)}, u32[]{:S(2)}) %copy-start.4) | copy-done | bytes 131096
  6.3 0.0 copy-start.5
  6.3 0.9 %copy-done.5 = f32[512,64]{0,1:T(8,128)S(1)} copy-done((f32[512,64]{0,1:T(8,128)S(1)}, f32[512,64]{0,1:T(8,128)}, u32[]{:S(2)}) %copy-start.5) | copy-done | bytes 131096
  7.2 0.0 copy-start.6
  7.2 0.9 %copy-done.6 = f32[512,64]{0,1:T(8,128)S(1)} copy-done((f32[512,64]{0,1:T(8,128)S(1)}, f32[512,64]{0,1:T(8,128)}, u32[]{:S(2)}) %copy-start.6) | copy-done | bytes 131096
  8.1 0.0 copy-start.7
  8.1 0.9 %copy-done.7 = f32[512,64]{0,1:T(8,128)S(1)} copy-done((f32[512,64]{0,1:T(8,128)S(1)}, f32[512,64]{0,1:T(8,128)}, u32[]{:S(2)}) %copy-start.7) | copy-done | bytes 131096
  9.0 0.8 %copy-done.8 = f32[64,64]{1,0:T(8,128)S(1)} copy-done((f32[64,64]{1,0:T(8,128)S(1)}, f32[64,64]{1,0:T(8,128)}, u32[]{:S(2)}) %copy-start.8) | copy-done | bytes 16408
  9.8 0.8 %copy-done.9 = f32[64,128]{1,0:T(8,128)S(1)} copy-done((f32[64,128]{1,0:T(8,128)S(1)}, f32[64,128]{1,0:T(8,128)}, u32[]{:S(2)}) %copy-start.9) | copy-done | bytes 32792
  10.6 0.8 %copy-done.10 = f32[64,64]{1,0:T(8,128)S(1)} copy-done((f32[64,64]{1,0:T(8,128)S(1)}, f32[64,64]{1,0:T(8,128)}, u32[]{:S(2)}) %copy-start.10) | copy-done | bytes 16408
  11.3 0.7 %copy-done.11 = s32[3]{0:T(128)S(1)} copy-done((s32[3]{0:T(128)S(1)}, s32[3]{0:T(128)}, u32[]{:S(2)}) %copy-start.11) | copy-done | bytes 36
  12.0 36.4 %shard_map.147 = (f32[64,64]{1,0:T(8,128)S(1)}, f32[64,512]{1,0:T(8,128)S(1)}, f32[64,512]{1,0:T(8,128)S(1)}, f32[1024,64]{1,0:T(8,128)S(1)}) custom-call(s32[3]{0:T(128)S(1)} %copy-done.11, f32[3,512,512]{2,1,0:T(8,128)S(1)} %bitcast.10, f32[64,64]{1,0:T(8,128)S(1)} %copy-done.8, f32[64,512]{1,0:T(8,128)S(1)} %bitcast.13, f32[64,512]{1,0:T(8,128)S(1)} %bitcast.14, ...), custom_call_target="tpu_custom_call" | custom-call | tf_op jit(solution)/shard_map/pallas_call | solution.py:420
  48.3 0.6 %copy.20 = f32[64,64]{1,0:T(8,128)} copy(f32[64,64]{1,0:T(8,128)S(1)} %get-tuple-element.16) | data formatting | bytes 32768
  49.0 0.7 %copy.21 = f32[512,64]{0,1:T(8,128)} copy(f32[512,64]{0,1:T(8,128)S(1)} %bitcast.19) | data formatting | bytes 262144
  49.6 0.7 %copy.22 = f32[512,64]{0,1:T(8,128)} copy(f32[512,64]{0,1:T(8,128)S(1)} %bitcast.18) | data formatting | bytes 262144
  50.3 0.8 %copy.23 = f32[32,32,64]{2,1,0:T(8,128)} copy(f32[32,32,64]{2,1,0:T(8,128)S(1)} %bitcast.12) | data formatting | bytes 524288
  (5 shorter events, 0.0 us)
Async XLA Ops:
  0.6 1.9 %copy-start = (f32[3,8,64,512]{3,2,1,0:T(8,128)S(1)}, f32[3,8,64,512]{3,2,1,0:T(8,128)}, u32[]{:S(2)}) copy-start(f32[3,8,64,512]{3,2,1,0:T(8,128)} %param.12) | copy-start | bytes 9437188
  2.5 1.0 %copy-start.1 = (f32[32,32,64]{2,1,0:T(8,128)S(1)}, f32[32,32,64]{2,1,0:T(8,128)}, u32[]{:S(2)}) copy-start(f32[32,32,64]{2,1,0:T(8,128)} %param.23) | copy-start | bytes 786436
  3.6 0.9 %copy-start.2 = (f32[512,128]{1,0:T(8,128)S(1)}, f32[512,128]{1,0:T(8,128)}, u32[]{:S(2)}) copy-start(f32[512,128]{1,0:T(8,128)} %phi_y.1) | copy-start | bytes 786436
  4.5 0.9 %copy-start.3 = (f32[512,64]{0,1:T(8,128)S(1)}, f32[512,64]{0,1:T(8,128)}, u32[]{:S(2)}) copy-start(f32[512,64]{0,1:T(8,128)} %param.15) | copy-start | bytes 393220
  5.4 0.9 %copy-start.4 = (f32[512,64]{0,1:T(8,128)S(1)}, f32[512,64]{0,1:T(8,128)}, u32[]{:S(2)}) copy-start(f32[512,64]{0,1:T(8,128)} %param.16) | copy-start | bytes 393220
  6.3 0.9 %copy-start.5 = (f32[512,64]{0,1:T(8,128)S(1)}, f32[512,64]{0,1:T(8,128)}, u32[]{:S(2)}) copy-start(f32[512,64]{0,1:T(8,128)} %param.19) | copy-start | bytes 393220
  7.2 0.9 %copy-start.6 = (f32[512,64]{0,1:T(8,128)S(1)}, f32[512,64]{0,1:T(8,128)}, u32[]{:S(2)}) copy-start(f32[512,64]{0,1:T(8,128)} %param.21) | copy-start | bytes 393220
  8.1 0.9 %copy-start.7 = (f32[512,64]{0,1:T(8,128)S(1)}, f32[512,64]{0,1:T(8,128)}, u32[]{:S(2)}) copy-start(f32[512,64]{0,1:T(8,128)} %param.22) | copy-start | bytes 393220
  9.0 0.8 %copy-start.8 = (f32[64,64]{1,0:T(8,128)S(1)}, f32[64,64]{1,0:T(8,128)}, u32[]{:S(2)}) copy-start(f32[64,64]{1,0:T(8,128)} %omega_x.1) | copy-start | bytes 49156
  9.8 0.8 %copy-start.9 = (f32[64,128]{1,0:T(8,128)S(1)}, f32[64,128]{1,0:T(8,128)}, u32[]{:S(2)}) copy-start(f32[64,128]{1,0:T(8,128)} %phi_x.1) | copy-start | bytes 98308
  10.6 0.8 %copy-start.10 = (f32[64,64]{1,0:T(8,128)S(1)}, f32[64,64]{1,0:T(8,128)}, u32[]{:S(2)}) copy-start(f32[64,64]{1,0:T(8,128)} %sketch_x.1) | copy-start | bytes 49156
  11.3 0.7 %copy-start.11 = (s32[3]{0:T(128)S(1)}, s32[3]{0:T(128)}, u32[]{:S(2)}) copy-start(s32[3]{0:T(128)} %index.1) | copy-start | bytes 40

commit v2 on v0

--- a/solution.py
+++ b/solution.py
@@ -1,28 +1,409 @@
+import functools
+
 import jax
 import jax.numpy as jnp
 from jax import lax
+from jax.experimental import pallas as pl
+from jax.experimental.pallas import tpu as pltpu
 from jax.sharding import PartitionSpec as P
 
 DZ = 16
+F32 = jnp.float32
+BF16 = jnp.bfloat16
+LANES = 128
+NN = (((1,), (0,)), ((), ()))
+NT = (((1,), (1,)), ((), ()))
 
 
 def contract(form, left, right):
     return jnp.einsum(form, left, right, precision=lax.Precision.HIGHEST)
 
 
-def shards(
-    slabs,
-    slab_index,
-    omega_x,
-    omega_y,
-    omega_z,
-    phi_x,
-    phi_y,
-    phi_z,
-    sketch_x,
-    sketch_y,
-    sketch_z,
-    core,
+def split(value):
+    high = value.astype(BF16)
+    return high, (value - high.astype(F32)).astype(BF16)
+
+
+def mul(left, right, dims=NN):
+    return lax.dot_general(left, right, dims, preferred_element_type=F32)
+
+
+def mul3(left_high, left_low, right_high, right_low, dims=NN):
+    rows = left_high.shape[0]
+    both = mul(jnp.concatenate([left_high, left_low], axis=0), right_high, dims)
+    return both[:rows] + both[rows:] + mul(left_high, right_low, dims)
+
+
+def iota(shape, dim):
+    return lax.broadcasted_iota(jnp.int32, shape, dim)
+
+
+def fused(
+    steps, planes, rows, row_width, col_width,
+    steps_at, slabs, omega_x, omega_y, omega_z, phi_x, phi_y, phi_z, sketch_x, sketch_y, sketch_z, core,
+    o_x, o_y, o_z, o_core,
+    index, v_slabs, v_ox, v_oy, v_oz, v_px, v_py, v_pz, v_sx, v_sy, v_sz, v_core, in_sem,
+    gy_out, gy_in, cols, px_in, raw_in, keep, mid_in, near_in, far_in, total, wa_in,
+    mix, parts, row_mix, own_high, own_low, far_high, far_low, y_sum, x_sum, z_sum, hot, depth,
+    y_in, xz_out, xz_in, x_out, x_in, rs_out, rs_in, ag_out, ag_all, ag_in, cube,
+    send_sem, recv_sem,
+):
+    gx, gy, wa = lax.axis_index("gx"), lax.axis_index("gy"), lax.axis_index("wa")
+    pair = gx + 1 - 2 * lax.rem(gx, 2)
+    across = 3 - gx
+    beyond = 3 - pair
+    inner = jnp.logical_or(gx == 1, gx == 2)
+    outer = jnp.logical_not(inner)
+    group = LANES // row_width
+    quads = planes // group
+    chunks = steps * quads
+    size = group * rows
+    flat = planes * rows
+    full = v_px.shape[1]
+    rank = v_oy.shape[0]
+    half, fold = rank // 2, rank // 4
+    n_sems = [0]
+
+    def local(src, dst, sem):
+        return pltpu.make_async_copy(src, dst, sem)
+
+    sources = (phi_y, omega_y, omega_z, omega_x, phi_x, phi_z, sketch_x, sketch_y, sketch_z, core)
+    places = (v_py, v_oy, v_oz, v_ox, v_px, v_pz, v_sx, v_sy, v_sz, v_core)
+    loads = [local(s, d, in_sem.at[k]) for k, (s, d) in enumerate(zip(sources, places))]
+    index_load = local(steps_at, index, in_sem.at[len(loads)])
+    fields = []
+    for c in range(chunks):
+        part = (c // quads, pl.ds(c % quads * size, size))
+        fields.append(local(slabs.at[part], v_slabs.at[part], in_sem.at[len(loads) + 1 + c]))
+    for copy in loads[:2] + fields[:2] + [index_load] + loads[2:6] + fields[2:] + loads[6:]:
+        copy.start()
+
+    barrier = pltpu.get_barrier_semaphore()
+    peers = [{"wa": 1 - wa}, {"gy": 1 - gy}, {"gx": pair}, {"gx": across}, {"gx": beyond}]
+    for where in peers:
+        pl.semaphore_signal(barrier, inc=1, device_id=where, device_id_type=pl.DeviceIdType.MESH)
+
+    def remote(src, dst, where):
+        k = n_sems[0]
+        n_sems[0] += 1
+        return pltpu.make_async_remote_copy(
+            src_ref=src, dst_ref=dst, send_sem=send_sem.at[k], recv_sem=recv_sem.at[k],
+            device_id=where, device_id_type=pl.DeviceIdType.MESH,
+        )
+
+    every = range(chunks)
+
+    def block(c, k):
+        return keep.at[c, :, pl.ds(k * LANES, LANES)]
+
+    to_gy = [remote(gy_out.at[c], gy_in.at[c], {"gy": 1 - gy}) for c in every]
+    to_px = remote(v_px, px_in, {"gx": pair})
+    to_raw = [remote(cols.at[c], raw_in.at[c], {"gx": pair}) for c in every]
+    to_near = [remote(block(c, 1), near_in.at[c], {"gx": pair}) for c in every]
+    to_mid = [remote(block(c, 2), mid_in.at[c], {"gx": across}) for c in every]
+    to_far = [remote(block(c, 3), far_in.at[c], {"gx": beyond}) for c in every]
+    to_wa = [remote(total.at[c], wa_in.at[c], {"wa": 1 - wa}) for c in every]
+    y_other = pl.ds(pl.multiple_of((1 - wa) * half, half), half)
+    y_own = pl.ds(pl.multiple_of(wa * half, half), half)
+    to_y = remote(y_sum.at[y_other], y_in, {"wa": 1 - wa})
+    to_xz = remote(xz_out, xz_in, {"gy": 1 - gy})
+    to_x = remote(x_out, x_in, {"wa": 1 - wa})
+    others = (pair, across, beyond)
+    to_rs = [remote(rs_out.at[o], rs_in.at[k], {"gx": o}) for k, o in enumerate(others)]
+    to_ag = [remote(ag_out, ag_all.at[gx], {"gx": o}) for o in others]
+    to_all = remote(ag_all, ag_in, {"wa": 1 - wa})
+
+    loads[0].wait()
+    loads[1].wait()
+    for k, part in enumerate(split(jnp.concatenate([v_py[...].T, v_oy[...]], axis=0))):
+        mix[k] = part
+
+    def stage_a(c):
+        fields[c].wait()
+        part = (c // quads, pl.ds(c % quads * size, size))
+        x_high, x_low = split(v_slabs[part])
+        parts[0, c * size:(c + 1) * size, :] = x_high
+        parts[1, c * size:(c + 1) * size, :] = x_low
+        mixed = mul3(mix[0], mix[1], x_high, x_low, NT)
+        for k in range(2):
+            @pl.when(gy == k)
+            def _():
+                cols[c] = mixed[k * col_width:(k + 1) * col_width]
+                gy_out[c] = mixed[(1 - k) * col_width:(2 - k) * col_width]
+        row_mix[:, c * size:(c + 1) * size] = mixed[full:]
+        if c == 0:
+            pl.semaphore_wait(barrier, len(peers))
+
+            @pl.when(outer)
+            def _():
+                loads[4].wait()
+                to_px.start()
+        to_gy[c].start()
+
+    depth_count = steps * planes
+
+    def rows_of(offsets):
+        lane = iota((v_oz.shape[1], LANES), 1)
+        wanted = jnp.full(lane.shape, -1, jnp.int32)
+        for k, offset in enumerate(offsets):
+            for t in range(steps):
+                first = k * depth_count + t * planes
+                inside = jnp.logical_and(lane >= first, lane < first + planes)
+                wanted = jnp.where(inside, lane - first + (index[t] * DZ + offset), wanted)
+        return (iota(lane.shape, 0) == wanted).astype(BF16)
+
+    def sketches(t, oz_high, oz_low, ox_tiles):
+        shape = (LANES, flat)
+        spread = (iota(shape, 0) == t * planes + iota(shape, 1) // rows).astype(BF16)
+        weight = mul(oz_high, spread) + mul(oz_low, spread)
+        w_high, w_low = split(weight * ox_tiles)
+        here = pl.ds(t * flat, flat)
+        y_part = mul3(w_high, w_low, parts[0, here, :], parts[1, here, :])
+        mixed = row_mix[:, here]
+        weighted = mixed * weight
+        x_part = functools.reduce(jnp.add, [weighted[:, k:k + LANES] for k in range(0, flat, LANES)])
+        m_high, m_low = split(mixed * ox_tiles)
+        z_part = mul(m_high, spread, NT) + mul(m_low, spread, NT)
+        for ref, part in ((y_sum, y_part), (x_sum, x_part), (z_sum, z_part)):
+            ref[...] = part if t == 0 else ref[...] + part
+
+    def blocks_of(phi, high_ref, low_ref):
+        phi_high, phi_low = split(phi)
+        k, l = iota((full, LANES), 0), iota((full, LANES), 1)
+        same = iota((size, LANES), 0) // rows == iota((size, LANES), 1) // row_width
+        for o, owner in enumerate((gx, pair, across, beyond)):
+            chosen = (k == owner * row_width + lax.rem(l, row_width)).astype(BF16)
+            for part, ref in ((phi_high, high_ref), (phi_low, low_ref)):
+                tiled = jnp.concatenate([mul(part, chosen)] * group, axis=0)
+                ref[:, o * LANES:(o + 1) * LANES] = jnp.where(same, tiled, 0.0).astype(BF16)
+
+    def stage_b(c):
+        to_gy[c].wait_recv()
+        cols[c] = cols[c] + gy_in[c]
+
+        @pl.when(outer)
+        def _():
+            to_raw[c].start()
+
+        @pl.when(inner)
+        def _():
+            high, low = split(cols[c])
+            keep[c] = mul3(high, low, own_high[...], own_low[...])
+
+    def stage_c(c):
+        @pl.when(inner)
+        def _():
+            to_raw[c].wait_recv()
+            high, low = split(raw_in[c])
+            keep[c] = keep[c] + mul3(high, low, far_high[...], far_low[...])
+            to_far[c].start()
+            to_mid[c].start()
+            to_near[c].start()
+
+    def stage_d(c):
+        @pl.when(inner)
+        def _():
+            to_mid[c].wait_recv()
+            total[c] = keep[c, :, :LANES] + mid_in[c]
+
+        @pl.when(outer)
+        def _():
+            to_near[c].wait_recv()
+            to_far[c].wait_recv()
+            total[c] = near_in[c] + far_in[c]
+
+        to_wa[c].start()
+        turn(0, c, total)
+
+    def turn(which, c, ref):
+        first = (which * chunks + c) * LANES
+        cube[first:first + LANES, :] = ref[c].T
+
+    def stage_f(c):
+        to_wa[c].wait_recv()
+        turn(1, c, wa_in)
+
+    def sums_1():
+        xz_out[:rank, :] = x_sum[...]
+        xz_out[rank:, :] = z_sum[...]
+        to_xz.start()
+        to_y.start()
+
+    def sums_2():
+        to_y.wait_recv()
+        to_xz.wait_recv()
+        y_half = y_sum[y_own, :] + y_in[...]
+        both = xz_out[...] + xz_in[...]
+        for k in range(4):
+            rs_out[k, :half, :] = y_half[:, k * LANES:(k + 1) * LANES]
+            rs_out[k, half:, :] = both[rank + k * fold:rank + (k + 1) * fold]
+        for copy in to_rs:
+            copy.start()
+        x_out[...] = both[:rank]
+        to_x.start()
+
+    def sums_3():
+        for copy in to_rs:
+            copy.wait_recv()
+        summed = rs_out[gx] + rs_in[0] + rs_in[1] + rs_in[2]
+        ag_out[...] = summed
+        for copy in to_ag:
+            copy.start()
+        ag_all[gx] = summed
+
+    def sums_4():
+        for copy in to_ag:
+            copy.wait_recv()
+        to_all.start()
+        to_x.wait_recv()
+        x_all = x_out[...] + x_in[...]
+        loads[6].wait()
+        o_x[...] = v_sx[...] + (x_all[:, :rows] + x_all[:, rows:]).T
+
+    def sums_5():
+        to_all.wait_recv()
+        loads[7].wait()
+        loads[8].wait()
+        for k in range(4):
+            lanes = slice(k * LANES, (k + 1) * LANES)
+            o_y[y_own, lanes] = v_sy[y_own, lanes] + ag_all[k, :half, :]
+            o_y[y_other, lanes] = v_sy[y_other, lanes] + ag_in[k, :half, :]
+        value = v_sz[...]
+        for ref, places in ((ag_all, hot[0]), (ag_in, hot[1])):
+            for part in split(jnp.concatenate([ref[k, half:, :] for k in range(4)], axis=0)):
+                value = value + mul(part, places, NT)
+        o_z[...] = value
+
+    stage_a(0)
+    stage_a(1)
+    index_load.wait()
+    for k in (2, 3, 5):
+        loads[k].wait()
+    hot[0] = rows_of((wa * planes, (1 - wa) * planes))
+    hot[1] = rows_of(((1 - wa) * planes,))
+    oz_high, oz_low = (mul(part, hot[0]).astype(BF16) for part in split(v_oz[...]))
+    ox_tiles = jnp.concatenate([v_ox[...].T] * planes, axis=1)
+    for c in range(2, chunks):
+        stage_a(c)
+
+    @pl.when(inner)
+    def _():
+        loads[4].wait()
+        blocks_of(v_px[...], own_high, own_low)
+        to_px.wait_recv()
+        blocks_of(px_in[...], far_high, far_low)
+
+    for t in range(steps):
+        stage_b(t)
+        sketches(t, oz_high, oz_low, ox_tiles)
+    sums_1()
+    for k, part in enumerate(split(v_pz[...])):
+        depth[k] = mul(part, hot[0])
+    stage_c(0)
+    stage_c(1)
+    extra = [sums_2, sums_3, sums_4, sums_5]
+    for c in range(steps, chunks + 4):
+        if c < chunks:
+            stage_b(c)
+        if c - 1 < chunks:
+            stage_c(c - 1)
+        if extra:
+            extra.pop(0)()
+        if 0 <= c - 3 < chunks:
+            stage_d(c - 3)
+        if 0 <= c - 4 < chunks:
+            stage_f(c - 4)
+    for action in extra:
+        action()
+
+    loads[9].wait()
+    owned = v_pz.shape[0] // 2
+    count = 2 * depth_count
+    spot = pl.ds(pl.multiple_of(wa * owned, owned), owned)
+    p_high, p_low = (depth[k, spot, :][:, :count].astype(BF16) for k in range(2))
+    for a in range(row_width):
+        high, low = split(cube[pl.ds(a, count, stride=row_width), :])
+        spot = pl.ds(a, owned, stride=row_width)
+        o_core[spot, :] = v_core[spot, :] + mul3(p_high, p_low, high, low)
+
+    for copy in to_gy + to_wa + [to_y, to_xz, to_x, to_all] + to_rs + to_ag:
+        copy.wait_send()
+
+    @pl.when(outer)
+    def _():
+        for copy in to_raw + [to_px]:
+            copy.wait_send()
+
+    @pl.when(inner)
+    def _():
+        for copy in to_near + to_mid + to_far:
+            copy.wait_send()
+
+
+def hand_over(*refs):
+    for source, place in zip(refs[:4], refs[4:]):
+        place[...] = source[...]
+
+
+def one_kernel(
+    slabs, slab_index, omega_x, omega_y, omega_z, phi_x, phi_y, phi_z, sketch_x, sketch_y, sketch_z, core
+):
+    steps, planes, rows, width = slabs.shape
+    rank, full = omega_x.shape[1], phi_x.shape[1]
+    row_width, col_width = core.shape[1], core.shape[2]
+    group = LANES // row_width
+    chunks = steps * planes // group
+    size = group * rows
+    half, fold = rank // 2, rank // 4
+    vmem = lambda shape, kind=F32: pltpu.VMEM(shape, kind)
+    like = lambda value: vmem(value.shape)
+    flat_core = core.reshape(-1, col_width)
+    operands = (
+        slabs.reshape(steps, planes * rows, width), omega_x, omega_y.T, omega_z.T, phi_x, phi_y, phi_z.T,
+        sketch_x, sketch_y.T, sketch_z.T, flat_core,
+    )
+    scratch = [pltpu.SMEM(slab_index.shape, jnp.int32)] + [like(value) for value in operands]
+    scratch += [
+        pltpu.SemaphoreType.DMA((11 + chunks,)),
+        *(vmem((chunks, col_width, size)) for _ in range(3)),
+        vmem((rows, full)), vmem((chunks, col_width, size)),
+        vmem((chunks, col_width, 4 * LANES)),
+        *(vmem((chunks, col_width, LANES)) for _ in range(5)),
+        vmem((2, full + rank, width), BF16), vmem((2, chunks * size, width), BF16), vmem((rank, chunks * size)),
+        *(vmem((size, 4 * LANES), BF16) for _ in range(4)),
+        vmem((rank, width)), vmem((rank, LANES)), vmem((rank, LANES)),
+        vmem((2, omega_z.shape[0], LANES), BF16), vmem((2, phi_z.shape[1], LANES)),
+        vmem((half, width)), vmem((2 * rank, LANES)), vmem((2 * rank, LANES)),
+        vmem((rank, LANES)), vmem((rank, LANES)),
+        vmem((4, half + fold, LANES)), vmem((3, half + fold, LANES)), vmem((half + fold, LANES)),
+        vmem((4, half + fold, LANES)), vmem((4, half + fold, LANES)),
+        vmem((2 * steps * planes * row_width, col_width)),
+        pltpu.SemaphoreType.DMA((7 * chunks + 11,)),
+        pltpu.SemaphoreType.DMA((7 * chunks + 11,)),
+    ]
+    outs = [jax.ShapeDtypeStruct(v.shape, F32) for v in operands[-4:]]
+    results = pl.pallas_call(
+        functools.partial(fused, steps, planes, rows, row_width, col_width),
+        out_shape=outs,
+        in_specs=[pl.BlockSpec(memory_space=pltpu.HBM)] * (1 + len(operands)),
+        out_specs=[pl.BlockSpec(memory_space=pltpu.VMEM)] * 4,
+        scratch_shapes=scratch,
+        compiler_params=pltpu.CompilerParams(
+            collective_id=0, has_side_effects=True, vmem_limit_bytes=60 * 2 ** 20
+        ),
+    )(slab_index, *operands)
+    new_x, new_y, new_z, new_core = pl.pallas_call(
+        hand_over,
+        out_shape=outs,
+        in_specs=[pl.BlockSpec(memory_space=pltpu.VMEM)] * 4,
+        out_specs=[pl.BlockSpec(memory_space=pltpu.VMEM)] * 4,
+        compiler_params=pltpu.CompilerParams(vmem_limit_bytes=60 * 2 ** 20),
+    )(*results)
+    return new_x, new_y.T, new_z.T, new_core.reshape(core.shape)
+
+
+def by_collectives(
+    slabs, slab_index, omega_x, omega_y, omega_z, phi_x, phi_y, phi_z, sketch_x, sketch_y, sketch_z, core
 ):
     planes = slabs.shape[1]
     x_parts = lax.axis_size("gx")
@@ -60,6 +441,8 @@
 
 
 def solution(mesh):
+    shape = dict(mesh.shape)
+    in_kernel = (shape["gx"], shape["gy"], shape["wa"]) == (4, 2, 2)
     placed = (
         P("runs", "wa", "gx", "gy"),
         P("runs"),
@@ -75,7 +458,7 @@
         P(("runs", "wa"), "gx", "gy"),
     )
     return jax.shard_map(
-        shards,
+        one_kernel if in_kernel else by_collectives,
         mesh=mesh,
         in_specs=placed,
         out_specs=(

time: 265 us -> 37 us (0.14)
  waiting for transfers between devices: 120 us -> 0 us
  blocking collectives: 51.7 us -> 0 us
  matrix products: 37 us -> 0 us
  Pallas kernels: 0 us -> 35.6 us
  local copies, waits for them, and re-layouts: 31 us -> 0 us
  between operations: 17.8 us -> 0.64 us
  other arithmetic: 5.28 us -> 0 us
    reduce_scatter x6 -> x0, waiting for transfers between devices: 120 us -> none  [the longest x3 104 us: shards(): lax.psum_scatter(blocks, ('gx', 'gy'), scatter_dimension=0, tiled=True)]
    psum x2 -> x0, blocking collectives: 46.3 us -> none  [the longest x1 35.2 us: shards(): plane_total = lax.psum(plane_part, ('gx', 'gy'))]
    dot_general x18 -> x0, matrix products: 37 us -> none  [contract(): return jnp.einsum(form, left, right, precision=lax.Precision.HIGHEST)]
    pallas_call x0 -> x2, Pallas kernels: none -> 35.6 us  [the longest x1 33.5 us: one_kernel(): pl.pallas_call(functools.partial(fused, steps, planes, rows, row_width, c...]
    transpose x7 -> x0, local copies, waits for them, and re-layouts: 13.9 us -> none  [the longest x3 7.08 us: shards(): blocks.transpose(1, 3, 0, 2, 4)]
    reshape x3 -> x0, local copies, waits for them, and re-layouts: 7.89 us -> none  [shards(): blocks = core_both.reshape(planes, x_parts, row_width, y_parts, col_width)]
    unnamed x38 -> x0, local copies, waits for them, and re-layouts: 7.07 us -> none
    all_gather x3 -> x0, blocking collectives: 5.35 us -> none  [shards(): slab_rows = lax.all_gather(plane_total, 'wa', axis=0, tiled=True)]
  transfers between devices with their start and end apart: 7 -> 0, of which waited for: 5 -> 0; matrix products, arithmetic and copies ran while one was open for 22% -> 0% of each run, Pallas kernels for 0% -> 0%
where the time goes in v2:
time: 37 us; the launch traced here: 36.3 us
  Pallas kernels  35.6 us (96%)
  between operations  0.64 us (2%)
    pallas_call x1, Pallas kernels, one_kernel(): pl.pallas_call(functools.partial(fused, steps, planes, rows, row_width, c...  33.5 us
    pallas_call x1, Pallas kernels, one_kernel(): pl.pallas_call(hand_over, out_shape=outs, in_specs=[pl.BlockSpec(memory_s...  2.1 us

profile of v2, /device:TPU:0, one launch (start us, length us, event | category | flops | bytes accessed | tf_op | source)
XLA Modules:
  0.0 36.3 jit_solution(4770437947560860118)
XLA Ops:
  0.6 33.5 %shard_map.147 = (f32[64,64]{1,0:T(8,128)}, f32[64,512]{1,0:T(8,128)}, f32[64,512]{1,0:T(8,128)}, f32[1024,64]{1,0:T(8,128)}) custom-call(s32[3]{0:T(128)} %steps_at.1, f32[3,512,512]{2,1,0:T(8,128)} %bitcast.10, f32[64,64]{1,0:T(8,128)} %omega_x.1, f32[64,512]{1,0:T(8,128)} %bitcast.12, f32[64,512]{1,0:T(8,128)} %bitcast.13, f32[64,128]{1,0:T(8,128)} %phi_x.1, ...), custom_call_target="tpu_custom_call" | custom-call | tf_op jit(solution)/shard_map/pallas_call | solution.py:385
  34.2 2.1 %shard_map.148 = (f32[64,64]{1,0:T(8,128)}, f32[64,512]{1,0:T(8,128)}, f32[64,512]{1,0:T(8,128)}, f32[1024,64]{1,0:T(8,128)}) custom-call(f32[64,64]{1,0:T(8,128)} %get-tuple-element.12.refs_0_, f32[64,512]{1,0:T(8,128)} %get-tuple-element.13.refs_1_, f32[64,512]{1,0:T(8,128)} %get-tuple-element.14.refs_2_, f32[1024,64]{1,0:T(8,128)} %get-tuple-element.15.refs_3_), custom_call_target="tpu_custom_call" | custom-call | tf_op jit(solution)/shard_map/pallas_call | solution.py:395

commit v3 on v2

--- a/solution.py
+++ b/solution.py
@@ -45,7 +45,7 @@
     index, v_slabs, v_ox, v_oy, v_oz, v_px, v_py, v_pz, v_sx, v_sy, v_sz, v_core, in_sem,
     gy_out, gy_in, cols, px_in, raw_in, keep, mid_in, near_in, far_in, total, wa_in,
     mix, parts, row_mix, own_high, own_low, far_high, far_low, y_sum, x_sum, z_sum, hot, depth,
-    y_in, xz_out, xz_in, x_out, x_in, rs_out, rs_in, ag_out, ag_all, ag_in, cube,
+    y_in, xz_out, xz_in, x_out, x_in, rs_out, rs_in, ag_out, ag_all, ag_in, z_out, z_in, z_own, z_far, cube,
     send_sem, recv_sem,
 ):
     gx, gy, wa = lax.axis_index("gx"), lax.axis_index("gy"), lax.axis_index("wa")
@@ -112,11 +112,15 @@
     to_rs = [remote(rs_out.at[o], rs_in.at[k], {"gx": o}) for k, o in enumerate(others)]
     to_ag = [remote(ag_out, ag_all.at[gx], {"gx": o}) for o in others]
     to_all = remote(ag_all, ag_in, {"wa": 1 - wa})
+    to_z = [remote(z_out, z_in.at[k], {"gx": o}) for k, o in enumerate(others)]
+    to_zw = remote(z_own, z_far, {"wa": 1 - wa})
 
     loads[0].wait()
     loads[1].wait()
     for k, part in enumerate(split(jnp.concatenate([v_py[...].T, v_oy[...]], axis=0))):
         mix[k] = part
+
+    held = max(chunks - 2, 1)
 
     def stage_a(c):
         fields[c].wait()
@@ -138,7 +142,8 @@
             def _():
                 loads[4].wait()
                 to_px.start()
-        to_gy[c].start()
+        if c < held:
+            to_gy[c].start()
 
     depth_count = steps * planes
 
@@ -223,26 +228,42 @@
         to_wa[c].wait_recv()
         turn(1, c, wa_in)
 
+    def moved(value, start):
+        shape = (LANES, LANES)
+        back, ahead = (0, start) if start >= 0 else (-start, 0)
+        source, place = iota(shape, 0) - back, iota(shape, 1) - ahead
+        same = jnp.logical_and(source == place, jnp.logical_and(source >= 0, source < LANES // 4))
+        high, low = split(value)
+        return mul(high, same.astype(BF16)) + mul(low, same.astype(BF16))
+
     def sums_1():
+        to_y.start()
         xz_out[:rank, :] = x_sum[...]
-        xz_out[rank:, :] = z_sum[...]
+        xz_out[rank:, :] = functools.reduce(
+            jnp.add, [moved(z_sum[k * fold:(k + 1) * fold, :], k * LANES // 4) for k in range(4)]
+        )
         to_xz.start()
-        to_y.start()
-
-    def sums_2():
+        for c in range(held, chunks):
+            to_gy[c].start()
+
+    def sums_y1():
         to_y.wait_recv()
+        y_half = y_sum[y_own, :] + y_in[...]
+        for k in range(4):
+            rs_out[k] = y_half[:, k * LANES:(k + 1) * LANES]
+        for copy in to_rs:
+            copy.start()
+
+    def sums_xz():
         to_xz.wait_recv()
-        y_half = y_sum[y_own, :] + y_in[...]
         both = xz_out[...] + xz_in[...]
-        for k in range(4):
-            rs_out[k, :half, :] = y_half[:, k * LANES:(k + 1) * LANES]
-            rs_out[k, half:, :] = both[rank + k * fold:rank + (k + 1) * fold]
-        for copy in to_rs:
+        z_out[...] = both[rank:]
+        for copy in to_z:
             copy.start()
         x_out[...] = both[:rank]
         to_x.start()
 
-    def sums_3():
+    def sums_y2():
         for copy in to_rs:
             copy.wait_recv()
         summed = rs_out[gx] + rs_in[0] + rs_in[1] + rs_in[2]
@@ -251,28 +272,36 @@
             copy.start()
         ag_all[gx] = summed
 
-    def sums_4():
-        for copy in to_ag:
+    def sums_z():
+        for copy in to_z:
             copy.wait_recv()
-        to_all.start()
+        z_own[...] = z_out[...] + z_in[0] + z_in[1] + z_in[2]
+        to_zw.start()
         to_x.wait_recv()
         x_all = x_out[...] + x_in[...]
         loads[6].wait()
         o_x[...] = v_sx[...] + (x_all[:, :rows] + x_all[:, rows:]).T
 
-    def sums_5():
+    def sums_y3():
+        for copy in to_ag:
+            copy.wait_recv()
+        to_all.start()
+
+    def sums_last():
+        to_zw.wait_recv()
+        loads[8].wait()
+        value = v_sz[...]
+        for ref, places in ((z_own, hot[0]), (z_far, hot[1])):
+            whole = jnp.concatenate([moved(ref[...], -(k * LANES // 4)) for k in range(4)], axis=0)
+            for part in split(whole):
+                value = value + mul(part, places, NT)
+        o_z[...] = value
         to_all.wait_recv()
         loads[7].wait()
-        loads[8].wait()
         for k in range(4):
             lanes = slice(k * LANES, (k + 1) * LANES)
-            o_y[y_own, lanes] = v_sy[y_own, lanes] + ag_all[k, :half, :]
-            o_y[y_other, lanes] = v_sy[y_other, lanes] + ag_in[k, :half, :]
-        value = v_sz[...]
-        for ref, places in ((ag_all, hot[0]), (ag_in, hot[1])):
-            for part in split(jnp.concatenate([ref[k, half:, :] for k in range(4)], axis=0)):
-                value = value + mul(part, places, NT)
-        o_z[...] = value
+            o_y[y_own, lanes] = v_sy[y_own, lanes] + ag_all[k]
+            o_y[y_other, lanes] = v_sy[y_other, lanes] + ag_in[k]
 
     stage_a(0)
     stage_a(1)
@@ -294,27 +323,26 @@
         blocks_of(px_in[...], far_high, far_low)
 
     for t in range(steps):
-        stage_b(t)
         sketches(t, oz_high, oz_low, ox_tiles)
+        if t < steps - 1:
+            stage_b(t)
     sums_1()
     for k, part in enumerate(split(v_pz[...])):
         depth[k] = mul(part, hot[0])
-    stage_c(0)
-    stage_c(1)
-    extra = [sums_2, sums_3, sums_4, sums_5]
-    for c in range(steps, chunks + 4):
-        if c < chunks:
-            stage_b(c)
-        if c - 1 < chunks:
-            stage_c(c - 1)
-        if extra:
-            extra.pop(0)()
-        if 0 <= c - 3 < chunks:
-            stage_d(c - 3)
-        if 0 <= c - 4 < chunks:
-            stage_f(c - 4)
-    for action in extra:
-        action()
+
+    between = {1: sums_y1, 2: sums_xz, 3: sums_y2, 4: sums_z, 5: sums_y3, 6: sums_last}
+    first = steps - 1
+    for s in range(chunks + 4):
+        if first + s < chunks:
+            stage_b(first + s)
+        if s < chunks:
+            stage_c(s)
+        if s in between:
+            between[s]()
+        if 0 <= s - 2 < chunks:
+            stage_d(s - 2)
+        if 0 <= s - 3 < chunks:
+            stage_f(s - 3)
 
     loads[9].wait()
     owned = v_pz.shape[0] // 2
@@ -326,7 +354,7 @@
         spot = pl.ds(a, owned, stride=row_width)
         o_core[spot, :] = v_core[spot, :] + mul3(p_high, p_low, high, low)
 
-    for copy in to_gy + to_wa + [to_y, to_xz, to_x, to_all] + to_rs + to_ag:
+    for copy in to_gy + to_wa + [to_y, to_xz, to_x, to_all, to_zw] + to_rs + to_ag + to_z:
         copy.wait_send()
 
     @pl.when(outer)
@@ -373,13 +401,14 @@
         *(vmem((size, 4 * LANES), BF16) for _ in range(4)),
         vmem((rank, width)), vmem((rank, LANES)), vmem((rank, LANES)),
         vmem((2, omega_z.shape[0], LANES), BF16), vmem((2, phi_z.shape[1], LANES)),
-        vmem((half, width)), vmem((2 * rank, LANES)), vmem((2 * rank, LANES)),
+        vmem((half, width)), vmem((rank + fold, LANES)), vmem((rank + fold, LANES)),
         vmem((rank, LANES)), vmem((rank, LANES)),
-        vmem((4, half + fold, LANES)), vmem((3, half + fold, LANES)), vmem((half + fold, LANES)),
-        vmem((4, half + fold, LANES)), vmem((4, half + fold, LANES)),
+        vmem((4, half, LANES)), vmem((3, half, LANES)), vmem((half, LANES)),
+        vmem((4, half, LANES)), vmem((4, half, LANES)),
+        vmem((fold, LANES)), vmem((3, fold, LANES)), vmem((fold, LANES)), vmem((fold, LANES)),
         vmem((2 * steps * planes * row_width, col_width)),
-        pltpu.SemaphoreType.DMA((7 * chunks + 11,)),
-        pltpu.SemaphoreType.DMA((7 * chunks + 11,)),
+        pltpu.SemaphoreType.DMA((7 * chunks + 15,)),
+        pltpu.SemaphoreType.DMA((7 * chunks + 15,)),
     ]
     outs = [jax.ShapeDtypeStruct(v.shape, F32) for v in operands[-4:]]
     results = pl.pallas_call(

time: 37 us -> 33.2 us (0.90); the launches traced: 36.3 us -> 33.1 us
  Pallas kernels: 35.6 us -> 32.4 us
    pallas_call x1, Pallas kernels: 33.5 us -> 30.3 us  [one_kernel(): pl.pallas_call(functools.partial(fused, steps, planes, rows, row_width, c...]
where the time goes in v3:
time: 33.2 us; the launch traced here: 33.1 us
  Pallas kernels  32.4 us (98%)
  between operations  0.64 us (2%)
    pallas_call x1, Pallas kernels, one_kernel(): pl.pallas_call(functools.partial(fused, steps, planes, rows, row_width, c...  30.3 us
    pallas_call x1, Pallas kernels, one_kernel(): pl.pallas_call(hand_over, out_shape=outs, in_specs=[pl.BlockSpec(memory_s...  2.1 us

profile of v3, /device:TPU:0, one launch (start us, length us, event | category | flops | bytes accessed | tf_op | source)
XLA Modules:
  0.0 33.1 jit_solution(3998020263333013691)
XLA Ops:
  0.6 30.3 %shard_map.147 = (f32[64,64]{1,0:T(8,128)}, f32[64,512]{1,0:T(8,128)}, f32[64,512]{1,0:T(8,128)}, f32[1024,64]{1,0:T(8,128)}) custom-call(s32[3]{0:T(128)} %steps_at.1, f32[3,512,512]{2,1,0:T(8,128)} %bitcast.10, f32[64,64]{1,0:T(8,128)} %omega_x.1, f32[64,512]{1,0:T(8,128)} %bitcast.12, f32[64,512]{1,0:T(8,128)} %bitcast.13, f32[64,128]{1,0:T(8,128)} %phi_x.1, ...), custom_call_target="tpu_custom_call" | custom-call | tf_op jit(solution)/shard_map/pallas_call | solution.py:414
  31.0 2.1 %shard_map.148 = (f32[64,64]{1,0:T(8,128)}, f32[64,512]{1,0:T(8,128)}, f32[64,512]{1,0:T(8,128)}, f32[1024,64]{1,0:T(8,128)}) custom-call(f32[64,64]{1,0:T(8,128)} %get-tuple-element.12.refs_0_, f32[64,512]{1,0:T(8,128)} %get-tuple-element.13.refs_1_, f32[64,512]{1,0:T(8,128)} %get-tuple-element.14.refs_2_, f32[1024,64]{1,0:T(8,128)} %get-tuple-element.15.refs_3_), custom_call_target="tpu_custom_call" | custom-call | tf_op jit(solution)/shard_map/pallas_call | solution.py:424

commit v4 on v3

--- a/solution.py
+++ b/solution.py
@@ -330,7 +330,7 @@
     for k, part in enumerate(split(v_pz[...])):
         depth[k] = mul(part, hot[0])
 
-    between = {1: sums_y1, 2: sums_xz, 3: sums_y2, 4: sums_z, 5: sums_y3, 6: sums_last}
+    between = {0: sums_y1, 2: sums_xz, 3: sums_y2, 5: sums_z, 6: sums_y3, 8: sums_last}
     first = steps - 1
     for s in range(chunks + 4):
         if first + s < chunks:

time: 33.2 us -> 32.5 us (0.979)
  Pallas kernels: 32.4 us -> 31.7 us
    pallas_call x1, Pallas kernels: 30.3 us -> 29.6 us  [one_kernel(): pl.pallas_call(functools.partial(fused, steps, planes, rows, row_width, c...]
where the time goes in v4:
time: 32.5 us; the launch traced here: 32.4 us
  Pallas kernels  31.7 us (98%)
  between operations  0.64 us (2%)
    pallas_call x1, Pallas kernels, one_kernel(): pl.pallas_call(functools.partial(fused, steps, planes, rows, row_width, c...  29.6 us
    pallas_call x1, Pallas kernels, one_kernel(): pl.pallas_call(hand_over, out_shape=outs, in_specs=[pl.BlockSpec(memory_s...  2.1 us

profile of v4, /device:TPU:0, one launch (start us, length us, event | category | flops | bytes accessed | tf_op | source)
XLA Modules:
  0.0 32.4 jit_solution(3872543140626794948)
XLA Ops:
  0.6 29.6 %shard_map.147 = (f32[64,64]{1,0:T(8,128)}, f32[64,512]{1,0:T(8,128)}, f32[64,512]{1,0:T(8,128)}, f32[1024,64]{1,0:T(8,128)}) custom-call(s32[3]{0:T(128)} %steps_at.1, f32[3,512,512]{2,1,0:T(8,128)} %bitcast.10, f32[64,64]{1,0:T(8,128)} %omega_x.1, f32[64,512]{1,0:T(8,128)} %bitcast.12, f32[64,512]{1,0:T(8,128)} %bitcast.13, f32[64,128]{1,0:T(8,128)} %phi_x.1, ...), custom_call_target="tpu_custom_call" | custom-call | tf_op jit(solution)/shard_map/pallas_call | solution.py:414
  30.3 2.1 %shard_map.148 = (f32[64,64]{1,0:T(8,128)}, f32[64,512]{1,0:T(8,128)}, f32[64,512]{1,0:T(8,128)}, f32[1024,64]{1,0:T(8,128)}) custom-call(f32[64,64]{1,0:T(8,128)} %get-tuple-element.12.refs_0_, f32[64,512]{1,0:T(8,128)} %get-tuple-element.13.refs_1_, f32[64,512]{1,0:T(8,128)} %get-tuple-element.14.refs_2_, f32[1024,64]{1,0:T(8,128)} %get-tuple-element.15.refs_3_), custom_call_target="tpu_custom_call" | custom-call | tf_op jit(solution)/shard_map/pallas_call | solution.py:424
